TPU v7x, 128 devices: a whole 4x4x4 slice. The times are simulated.
128 devices in a mesh: dp: 16 (over y, z), section: 2 (over x_hi), mp: 4 (over x_lo, core).
Axes of the slice: x: 4 (x_hi: 2, x_lo: 2; x = x_hi * 2 + x_lo), y: 4, z: 4, core: 2. Of those that a mesh axis runs over, the one named last changes fastest.
Arguments:
- tokens: bfloat16 [16384, 4096], P(('dp', 'section')), may hold values from -8 to 8
- routes: int32 [16384, 8], P(('dp', 'section')), may hold values from 0 to 127, all different within a row; in each aligned block of 512 rows (0 to 511, 512 to 1023, ...) at most 64 rows name the same one
- weight: bfloat16 [2, 16, 4096, 1536], P('section', 'dp', None, 'mp')
- quantized: bfloat16 [2, 16, 4096, 1536], P('section', 'dp', None, 'mp')
Outputs:
- refit_scale: float32 [2, 16, 1536], P('section', 'dp', 'mp')
- refit_bias: float32 [2, 16, 1536], P('section', 'dp', 'mp')
Inputs may be any that keep to these rules, and one draw needn't show every extreme that they name: `routes`: each token names 8 different experts; the tokens of one device name any one expert at most 64 times.
All inputs are finite; a program needn't handle non-finite values.
Results may differ from a plain program's by a relative error of at most 0.0003.
Values may be sent and summed in bfloat16 or wider, within the bound.
A program may use at most 128 MiB of HBM per device.

v0:
```python
import jax
import jax.numpy as jnp
from jax import lax
from jax.sharding import PartitionSpec as P

CAP = 64


RIDGE = 1.0


def from_behind(block, axis, distance):
    devices = range(lax.axis_size(axis))
    route = [((i - distance) % len(devices), i) for i in devices]
    return lax.ppermute(block, axis, route)


def column_sums(row_block, weight_block, quant_block):
    full_out = jnp.einsum(
        "sekd,edf->sekf", row_block, weight_block, preferred_element_type=jnp.float32
    )
    quant_out = jnp.einsum(
        "sekd,edf->sekf", row_block, quant_block, preferred_element_type=jnp.float32
    )
    return jnp.stack(
        [
            jnp.sum(quant_out * quant_out, axis=(0, 2)),
            jnp.sum(quant_out, axis=(0, 2)),
            jnp.sum(quant_out * full_out, axis=(0, 2)),
            jnp.sum(full_out, axis=(0, 2)),
        ]
    )


def refit_columns(moments, counts):
    square = moments[0]
    first_moment = moments[1]
    cross_term = moments[2]
    target = moments[3]
    denominator = counts + RIDGE
    diagonal = square + RIDGE
    anchored = cross_term + RIDGE
    determinant = diagonal * denominator - first_moment * first_moment
    refit_scale = (denominator * anchored - first_moment * target) / determinant
    refit_bias = (diagonal * target - first_moment * anchored) / determinant
    return (refit_scale, refit_bias)


def local(tokens, routes, weight, quantized):
    owners = lax.axis_size("dp")
    per_owner = weight.shape[1]
    window = owners * per_owner
    token_total = tokens.shape[0]
    expert_iota = jnp.arange(window, dtype=jnp.int32)
    chosen = jnp.any(routes[:, :, None] == expert_iota[None, None, :], axis=1)
    chosen_int = chosen.astype(jnp.int32)
    local_counts = jnp.sum(chosen_int, axis=0)
    position = jnp.cumsum(chosen_int, axis=0) - 1
    slot_iota = jnp.arange(CAP, dtype=jnp.int32)
    matches = chosen[:, :, None] & (position[:, :, None] == slot_iota[None, None, :])
    token_iota = jnp.arange(token_total, dtype=jnp.int32)
    row_index = jnp.sum(jnp.where(matches, token_iota[:, None, None], 0), axis=0)
    occupied = jnp.any(matches, axis=0)
    slot_rows = jnp.where(occupied[:, :, None], tokens[row_index], jnp.zeros((), tokens.dtype))
    received = lax.all_to_all(slot_rows, "dp", split_axis=0, concat_axis=0, tiled=True)
    row_block = received.reshape(owners, per_owner, CAP, tokens.shape[1])
    totals = lax.psum(local_counts, ("dp", "section"))
    owned = lax.dynamic_slice_in_dim(totals, lax.axis_index("dp") * per_owner, per_owner)
    counts = owned.astype(jnp.float32)[:, None]
    other_rows = from_behind(row_block, "section", 1)
    moments = column_sums(row_block, weight[0], quantized[0]) + column_sums(
        other_rows, weight[0], quantized[0]
    )
    refit_scale, refit_bias = refit_columns(moments, counts)
    return (refit_scale[None], refit_bias[None])


def solution(mesh):
    placed = (
        P(("dp", "section"), None),
        P(("dp", "section"), None),
        P("section", "dp", None, "mp"),
        P("section", "dp", None, "mp"),
    )
    return jax.shard_map(
        local,
        mesh=mesh,
        in_specs=placed,
        out_specs=(P("section", "dp", "mp"), P("section", "dp", "mp")),
        check_vma=False,
    )
```

profile of v0, /device:TPU:1, one launch (start us, length us, event | category | flops | bytes accessed | tf_op | source)
XLA Modules:
  0.0 353.9 jit_solution(5177512372035921846)
XLA Ops:
  0.6 0.0 copy-start
  0.6 0.9 fusion.12
  1.6 1.2 reduce-window.6
  2.7 0.2 slice_reduce_fusion
  3.0 0.1 bitcast_bitcast_fusion
  3.1 0.4 fusion.11
  3.5 0.5 select_reduce_fusion
  4.0 0.1 reshape.257
  4.1 17.8 %gather_fusion = bf16[1024,4096]{1,0:T(8,128)(2,1)} fusion(bf16[512,4096]{1,0:T(8,128)(2,1)} %param.4, s32[1024]{0:T(1024)S(1)} %broadcast_clamp_fusion), kind=kCustom, calls=%fused_computation | custom fusion | bytes 16781312 | tf_op jit(solution)/shard_map/gather | solution.py:64
  21.9 7.2 %broadcast_select_fusion = bf16[16,64,4096]{2,1,0:T(8,128)(2,1)} fusion(bf16[16,64,4096]{2,1,0:T(8,128)(2,1)} %bitcast.47, pred[16,64]{1,0:T(8,128)(4,1)S(1)} %fusion.11), kind=kLoop, calls=%fused_computation.5 | loop fusion | flops 4194304 | bytes 16778240 | tf_op jit(solution)/shard_map/jit(_where)/select_n | solution.py:64
  29.1 103.4 %all_to_all.5 = bf16[16,64,4096]{2,1,0:T(8,128)(2,1)} all-to-all(bf16[16,64,4096]{2,1,0:T(8,128)(2,1)} %broadcast_select_fusion), channel_id=1, replica_groups=mesh['dp'=16,'section'=2,'mp'=4] {'dp'}, dimensions={0} | all-to-all | bytes 16777216 | tf_op jit(solution)/shard_map/all_to_all | solution.py:65
  132.5 2.7 collective-permute-start
  135.3 0.1 convert_reduce_fusion
  135.4 186.7 %psum.7 = s32[16]{0:T(128)S(1)} all-reduce(s32[16]{0:T(128)S(1)} %convert_reduce_fusion), channel_id=1, replica_groups=mesh['dp'=16,'section'=2,'mp'=4] {'dp','section'}, use_global_device_ids=true, to_apply=%region_2.0 | all-reduce | flops 16 | bytes 128 | tf_op jit(solution)/shard_map/psum | solution.py:67
  322.1 0.6 dynamic_slice.3
  323.4 0.0 copy-done
  323.4 0.0 copy-start.1
  323.4 7.0 %fusion.5 = f32[16,64,384]{2,1,0:T(8,128)S(1)} fusion(bf16[16,64,4096]{2,1,0:T(8,128)(2,1)} %all_to_all.5, bf16[1,1,4096,384]{3,2,1,0:T(8,128)(2,1)S(1)} %copy-done), kind=kOutput, calls=%fused_computation.7 | convolution fusion | flops 3221225472 | bytes 13107200 | tf_op jit(solution)/shard_map/sekd,edf->sekf/dot_general | solution.py:19
  330.4 0.0 copy-done.1
  330.4 7.9 %multiply_reduce_fusion.3 = (f32[384]{0:T(512)S(1)}, f32[384]{0:T(512)S(1)}, f32[384]{0:T(512)S(1)}, f32[384]{0:T(512)S(1)}) fusion(f32[16,64,384]{2,1,0:T(8,128)S(1)} %fusion.5, bf16[16,64,4096]{2,1,0:T(8,128)(2,1)} %all_to_all.5, bf16[1,1,4096,384]{3,2,1,0:T(8,128)(2,1)S(1)} %copy-done.1), kind=kOutput, calls=%fused_computation.19 | convolution fusion | flops 3223582720 | bytes 13113344 | tf_op jit(solution)/shard_map/sekd,edf->sekf/dot_general | solution.py:22
  338.4 0.0 collective-permute-done
  338.4 6.9 %fusion = f32[16,64,384]{2,1,0:T(8,128)S(1)} fusion(bf16[16,1,64,4096]{3,2,0,1:T(8,128)(2,1)} %collective-permute-done, bf16[1,1,4096,384]{3,2,1,0:T(8,128)(2,1)S(1)} %copy-done), kind=kOutput, calls=%fused_computation.1 | convolution fusion | flops 3221225472 | bytes 13107200 | tf_op jit(solution)/shard_map/sekd,edf->sekf/dot_general | solution.py:19
  345.3 7.9 %multiply_reduce_fusion.1 = (f32[384]{0:T(512)S(1)}, f32[384]{0:T(512)S(1)}, f32[384]{0:T(512)S(1)}, f32[384]{0:T(512)S(1)}) fusion(f32[16,64,384]{2,1,0:T(8,128)S(1)} %fusion, bf16[1,1,4096,384]{3,2,1,0:T(8,128)(2,1)S(1)} %copy-done.1, bf16[16,1,64,4096]{3,2,0,1:T(8,128)(2,1)} %collective-permute-done), kind=kOutput, calls=%fused_computation.17 | convolution fusion | flops 3223582720 | bytes 13113344 | tf_op jit(solution)/shard_map/sekd,edf->sekf/dot_general | solution.py:22
  353.3 0.6 subtract_divide_fusion
  (14 shorter events, 0.1 us)
Async XLA Ops:
  0.6 322.7 %copy-start = (bf16[1,1,4096,384]{3,2,1,0:T(8,128)(2,1)S(1)}, bf16[1,1,4096,384]{3,2,1,0:T(8,128)(2,1)}, u32[]{:S(2)}) copy-start(bf16[1,1,4096,384]{3,2,1,0:T(8,128)(2,1)} %param.6) | copy-start | bytes 9437188
  132.5 205.9 %collective-permute-start = (bf16[16,1,64,4096]{3,2,0,1:T(8,128)(2,1)}, bf16[16,1,64,4096]{3,2,0,1:T(8,128)(2,1)}, u32[]{:S(2)}, u32[]{:S(2)}) collective-permute-start(bf16[16,1,64,4096]{3,2,0,1:T(8,128)(2,1)} %bitcast.9), channel_id=1, source_target_pairs={{4,0},{0,4},{5,1},{1,5},{6,2},{2,6},{7,3},{3,7},{12,8},{8,12},{13,... | collective-permute-start | bytes 25165832 | tf_op jit(solution)/shard_map/ppermute | solution.py:15
  323.4 7.0 %copy-start.1 = (bf16[1,1,4096,384]{3,2,1,0:T(8,128)(2,1)S(1)}, bf16[1,1,4096,384]{3,2,1,0:T(8,128)(2,1)}, u32[]{:S(2)}) copy-start(bf16[1,1,4096,384]{3,2,1,0:T(8,128)(2,1)} %param.7) | copy-start | bytes 9437188
where the time goes:
time: 359 us; the launch traced here: 354 us
  blocking collectives  290 us (81%)
  matrix products  29.7 us (8%)
  local copies, waits for them, and re-layouts  18.7 us (5%)
  other arithmetic  11.1 us (3%)
    psum x1, blocking collectives, local(): totals = lax.psum(local_counts, ('dp', 'section'))  187 us
    all_to_all x1, blocking collectives, local(): lax.all_to_all(slot_rows, 'dp', split_axis=0, concat_axis=0, tiled=True)  103 us
    gather x1, local copies, waits for them, and re-layouts, local(): tokens[row_index]  17.8 us
    dot_general x2, matrix products, column_sums(): jnp.einsum('sekd,edf->sekf', row_block, quant_block, preferred_element_ty...  15.8 us
    dot_general x2, matrix products, column_sums(): jnp.einsum('sekd,edf->sekf', row_block, weight_block, preferred_element_t...  13.9 us
    select_n x1, other arithmetic, local(): jnp.where(occupied[:, :, None], tokens[row_index], jnp.zeros((), tokens.d...  7.22 us
  transfers between devices with their start and end apart: 1, of which 0 were waited for; matrix products, arithmetic and copies ran while one was open for 4% of the time, Pallas kernels for 0%

commit v1 on v0

v1 whole, which is shorter than its diff:
```python
import functools

import jax
import jax.numpy as jnp
from jax import lax
from jax.experimental import pallas as pl
from jax.experimental.pallas import tpu as pltpu
from jax.sharding import PartitionSpec as P

CAP = 64
RIDGE = 1.0
MESH = pl.DeviceIdType.MESH
SIDE = 4
SHIFTS = SIDE * SIDE
GROUP = SIDE * CAP


def kernel(
    tok_hbm,
    routes_ref,
    w_hbm,
    q_hbm,
    scale_ref,
    bias_ref,
    tok,
    wq,
    outbox,
    rows,
    places,
    acc,
    mom,
    tally,
    tally_in,
    tally_other,
    load_sem,
    a_send,
    a_recv,
    x_send,
    x_recv,
    f_send,
    f_recv,
    c_send,
    c_recv,
    d_send,
    d_recv,
    t_send,
    t_recv,
    u_sem,
):
    dp, section, mp = lax.axis_index("dp"), lax.axis_index("section"), lax.axis_index("mp")
    y, z = dp // SIDE, dp % SIDE
    x_lo, core = mp // 2, mp % 2
    half = tok.shape[1]
    token_total = tok.shape[0]
    columns = w_hbm.shape[-1]

    across = (dp, 1 - section, (1 - x_lo) * 2 + core)
    beside = (dp, section, (1 - x_lo) * 2 + core)
    twin = (dp, section, x_lo * 2 + 1 - core)
    mine = jnp.where(section == x_lo, 0, CAP // 2)
    theirs = CAP // 2 - mine

    def shift(k):
        dy = k % SIDE
        dz = (k // SIDE + k) % SIDE
        return ((y + dy) % SIDE) * SIDE + (z + dz) % SIDE

    def rows_at(region, k, start=0, size=CAP):
        first = pl.multiple_of((region * SHIFTS + k) * CAP + start, 16)
        return pl.ds(first, size)

    def a_copy(k):
        return pltpu.make_async_remote_copy(
            outbox.at[pl.ds(pl.multiple_of(k * CAP, CAP), CAP)],
            rows.at[core, rows_at(0, k)],
            a_send.at[k],
            a_recv.at[k],
            (shift(k), section, mp),
            MESH,
        )

    def t_copy(k):
        return pltpu.make_async_remote_copy(
            tally, tally_in.at[k], t_send.at[k], t_recv.at[k], (shift(k), section, mp), MESH
        )

    def x_copy(k):
        return pltpu.make_async_remote_copy(
            rows.at[core, rows_at(0, k, mine, CAP // 2)],
            rows.at[core, rows_at(1, k, mine, CAP // 2)],
            x_send.at[k],
            x_recv.at[k],
            across,
            MESH,
        )

    def f_copy(k, start):
        return pltpu.make_async_remote_copy(
            rows.at[core, rows_at(1, k, start, CAP // 2)],
            rows.at[core, rows_at(1, k, start, CAP // 2)],
            f_send.at[k],
            f_recv.at[k],
            beside,
            MESH,
        )

    def c_copy(k, owner):
        return pltpu.make_async_remote_copy(
            rows.at[owner, rows_at(0, k)],
            rows.at[owner, rows_at(0, k)],
            c_send.at[k],
            c_recv.at[k],
            twin,
            MESH,
        )

    def d_copy(k, owner):
        return pltpu.make_async_remote_copy(
            rows.at[owner, rows_at(1, k)],
            rows.at[owner, rows_at(1, k)],
            d_send.at[k],
            d_recv.at[k],
            twin,
            MESH,
        )

    loads = [
        pltpu.make_async_copy(
            tok_hbm.at[:, pl.ds(pl.multiple_of(core * half, half), half)], tok, load_sem.at[0]
        )
    ]
    for part in range(2):
        for i, source in enumerate((w_hbm, q_hbm)):
            loads.append(
                pltpu.make_async_copy(
                    source.at[0, 0, pl.ds(part * half, half)],
                    wq.at[part, :, pl.ds(i * columns, columns)],
                    load_sem.at[1 + 2 * part + i],
                )
            )
    for load in loads:
        load.start()

    barrier = pltpu.get_barrier_semaphore()
    for k in range(1, SHIFTS):
        pl.semaphore_signal(barrier, 1, device_id=(shift(k), section, mp), device_id_type=MESH)
    for peer in (across, beside, twin):
        pl.semaphore_signal(barrier, 1, device_id=peer, device_id_type=MESH)

    lanes = lax.broadcasted_iota(jnp.int32, (token_total, 128), 1)
    chosen = jnp.zeros((token_total, 128), jnp.float32)
    for i in range(routes_ref.shape[1]):
        chosen += jnp.where(routes_ref[:, i : i + 1] == lanes, 1.0, 0.0)
    before = lax.broadcasted_iota(jnp.int32, (token_total, token_total), 1)
    after = lax.broadcasted_iota(jnp.int32, (token_total, token_total), 0)
    lower = jnp.where(before <= after, 1.0, 0.0).astype(jnp.bfloat16)
    rank = jnp.dot(lower, chosen.astype(jnp.bfloat16), preferred_element_type=jnp.float32)
    tally[...] = jnp.broadcast_to(rank[token_total - 1 :], tally.shape)
    place = jnp.where(chosen > 0, rank - 1.0, -1.0)
    places[...] = jnp.transpose(place)
    mom[...] = jnp.zeros_like(mom)
    loads[0].wait()

    slot = lax.broadcasted_iota(jnp.int32, (CAP, token_total), 0).astype(jnp.float32)

    def collect(group):
        picks = []
        for j in range(SIDE):
            k = group * SIDE + j
            line = places[pl.ds(shift(k), 1), :]
            picks.append(jnp.where(line == slot, 1.0, 0.0).astype(jnp.bfloat16))
        pick = jnp.concatenate(picks, axis=0)
        first = pl.multiple_of(group * GROUP, GROUP)
        outbox[pl.ds(first, GROUP), :] = jnp.dot(
            pick, tok[...], preferred_element_type=jnp.float32
        ).astype(jnp.bfloat16)

    collect(0)
    rows[core, :CAP, :] = outbox[:CAP, :]
    pl.semaphore_wait(barrier, SHIFTS + 2)

    for k in range(1, SIDE):
        a_copy(k).start()
    x_copy(0).start()
    c_copy(0, core).start()
    for k in range(1, SHIFTS):
        t_copy(k).start()

    @pl.loop(1, SIDE)
    def _(group):
        collect(group)
        for j in range(SIDE):
            a_copy(group * SIDE + j).start()

    for load in loads[1:]:
        load.wait()

    def multiply(region, group):
        first = pl.multiple_of((region * SHIFTS + group * SIDE) * CAP, GROUP)
        acc[...] = jnp.dot(
            rows[0, pl.ds(first, GROUP), :], wq[0], preferred_element_type=jnp.float32
        ) + jnp.dot(rows[1, pl.ds(first, GROUP), :], wq[1], preferred_element_type=jnp.float32)
        full = acc[:, :columns]
        quant = acc[:, columns:]

        def fold(values):
            return jnp.sum(values.reshape(GROUP // 8, 8, columns), axis=0)

        mom[0] += fold(quant * quant)
        mom[1] += fold(quant)
        mom[2] += fold(quant * full)
        mom[3] += fold(full)

    def finish_own(group):
        for j in range(SIDE):
            c_copy(group * SIDE + j, 1 - core).wait_recv()
        multiply(0, group)

    def finish_other(group):
        for j in range(SIDE):
            d_copy(group * SIDE + j, 1 - core).wait_recv()
        multiply(1, group)

    def arrive(k):
        a_copy(k).wait_recv()
        x_copy(k).start()
        c_copy(k, core).start()

    def relay(k):
        x_copy(k).wait_recv()
        f_copy(k, mine).start()

    def hand(k):
        f_copy(k, theirs).wait_recv()
        d_copy(k, core).start()

    @pl.loop(0, SIDE)
    def _(group):
        for j in range(SIDE):
            k = group * SIDE + j
            if j:
                arrive(k)
                relay(k - 1)
                if j > 1:
                    hand(k - 2)
                else:
                    pl.when(group > 0)(lambda: hand(k - 2))
            else:

                @pl.when(group > 0)
                def _():
                    arrive(k)
                    relay(k - 1)
                    hand(k - 2)

        pl.when(group > 0)(lambda: finish_own(group - 1))
        pl.when(group > 1)(lambda: finish_other(group - 2))

    last = SHIFTS - 1
    relay(last)
    hand(last - 1)
    finish_own(SIDE - 1)
    hand(last)
    finish_other(SIDE - 2)

    total = tally[...]
    for k in range(1, SHIFTS):
        t_copy(k).wait_recv()
        total += tally_in[k]
    tally_in[0] = total
    u_copy = pltpu.make_async_remote_copy(
        tally_in.at[0], tally_other, u_sem.at[0], u_sem.at[1], across, MESH
    )
    u_copy.start()

    finish_other(SIDE - 1)

    u_copy.wait()
    total += tally_other[...]
    lane = lax.broadcasted_iota(jnp.int32, total.shape, 1)
    counts = jnp.sum(jnp.where(lane == dp, total, 0.0), axis=1, keepdims=True)[:1]

    square, first_moment, cross_term, target = (
        jnp.sum(mom[i], axis=0, keepdims=True) for i in range(4)
    )
    denominator = counts + RIDGE
    diagonal = square + RIDGE
    anchored = cross_term + RIDGE
    determinant = diagonal * denominator - first_moment * first_moment
    scale_ref[0] = (denominator * anchored - first_moment * target) / determinant
    bias_ref[0] = (diagonal * target - first_moment * anchored) / determinant

    @pl.loop(1, SHIFTS)
    def _(k):
        a_copy(k).wait_send()
        t_copy(k).wait_send()

    @pl.loop(0, SHIFTS)
    def _(k):
        x_copy(k).wait_send()
        f_copy(k, mine).wait_send()
        c_copy(k, core).wait_send()
        d_copy(k, core).wait_send()


def local(tokens, routes, weight, quantized):
    token_total, width = tokens.shape
    columns = weight.shape[-1]
    out = jax.ShapeDtypeStruct((1, 1, columns), jnp.float32)
    vmem = pl.BlockSpec(memory_space=pltpu.VMEM)
    hbm = pl.BlockSpec(memory_space=pl.ANY)
    sems = pltpu.SemaphoreType.DMA
    return pl.pallas_call(
        kernel,
        out_shape=(out, out),
        in_specs=[hbm, vmem, hbm, hbm],
        out_specs=(vmem, vmem),
        scratch_shapes=[
            pltpu.VMEM((token_total, width // 2), jnp.bfloat16),
            pltpu.VMEM((2, width // 2, 2 * columns), jnp.bfloat16),
            pltpu.VMEM((SHIFTS * CAP, width // 2), jnp.bfloat16),
            pltpu.VMEM((2, 2 * SHIFTS * CAP, width // 2), jnp.bfloat16),
            pltpu.VMEM((128, token_total), jnp.float32),
            pltpu.VMEM((GROUP, 2 * columns), jnp.float32),
            pltpu.VMEM((4, 8, columns), jnp.float32),
            pltpu.VMEM((8, 128), jnp.float32),
            pltpu.VMEM((SHIFTS, 8, 128), jnp.float32),
            pltpu.VMEM((8, 128), jnp.float32),
            sems((5,)),
        ]
        + [sems((SHIFTS,))] * 12
        + [sems((2,))],
        compiler_params=pltpu.CompilerParams(
            collective_id=0, has_side_effects=True, vmem_limit_bytes=56 << 20
        ),
        cost_estimate=pl.CostEstimate(
            flops=2 * 2048 * 4096 * 768, bytes_accessed=10 << 20, transcendentals=0
        ),
    )(tokens, routes, weight, quantized)


def solution(mesh):
    placed = (
        P(("dp", "section"), None),
        P(("dp", "section"), None),
        P("section", "dp", None, "mp"),
        P("section", "dp", None, "mp"),
    )
    return jax.shard_map(
        local,
        mesh=mesh,
        in_specs=placed,
        out_specs=(P("section", "dp", "mp"), P("section", "dp", "mp")),
        check_vma=False,
    )
```

time: 359 us -> 104 us (0.29)
  the two profiles are of different devices: /device:TPU:1 before, /device:TPU:72 now
where the time goes in v1:
time: 104 us
  Pallas kernels  99.5 us (96%)
  local copies, waits for them, and re-layouts  4.02 us (4%)
    pallas_call x1, Pallas kernels, local(): pl.pallas_call(kernel, out_shape=(out, out), in_specs=[hbm, vmem, hbm, hb...  99.5 us
    unnamed x3, local copies, waits for them, and re-layouts  4.02 us

profile of v1, /device:TPU:72, one launch (start us, length us, event | category | flops | bytes accessed | tf_op | source)
XLA Modules:
  0.0 104.1 jit_solution(10855602782115556689)
XLA Ops:
  0.6 1.5 %copy.6.routes_ref = s32[512,8]{1,0:T(8,128)} copy(s32[512,8]{0,1:T(8,128)} %param.5) | data formatting | bytes 32768 | tf_op args[1]
  2.2 99.5 %shard_map.59 = (f32[1,1,384]{2,1,0:T(1,128)}, f32[1,1,384]{2,1,0:T(1,128)}) custom-call(bf16[512,4096]{1,0:T(8,128)(2,1)} %tok_hbm.1, s32[512,8]{1,0:T(8,128)} %copy.6.routes_ref, bf16[1,1,4096,384]{3,2,1,0:T(8,128)(2,1)} %w_hbm.1, bf16[1,1,4096,384]{3,2,1,0:T(8,128)(2,1)} %q_hbm.1), custom_call_target="tpu_custom_call" | custom-call | flops 12884901888 | bytes 10485760 | tf_op jit(solution)/shard_map/pallas_call | solution.py:313
  101.7 1.2 %copy.9 = f32[1,1,384]{2,1,0:T(1,128)} copy(f32[1,1,384]{2,1,0:T(1,128)} %get-tuple-element.4) | data formatting | bytes 3072
  102.9 1.2 %copy.10 = f32[1,1,384]{2,1,0:T(1,128)} copy(f32[1,1,384]{2,1,0:T(1,128)} %get-tuple-element.5) | data formatting | bytes 3072

commit v2 on v0

v2 whole, which is shorter than its diff:
```python
import functools

import jax
import jax.numpy as jnp
from jax import lax
from jax.experimental import pallas as pl
from jax.experimental.pallas import tpu as pltpu
from jax.sharding import PartitionSpec as P

CAP = 64
RIDGE = 1.0
MESH = pl.DeviceIdType.MESH
SIDE = 4
SHIFTS = SIDE * SIDE
PIECE = CAP // 2
UNIT = PIECE // 2
GROUP = SIDE * PIECE
PRODUCTS = {
    2: (0,), 5: (8,), 6: (1,), 7: (12,), 9: (9,), 10: (2,), 11: (13,), 12: (4,), 13: (10,),
    14: (3, 5), 15: (14,), 16: (6,), 17: (11, 7), 18: (15,),
}
STEPS = 19
NEAREST = (
    (0, 0), (1, 0), (0, 1), (3, 0), (0, 3), (1, 1), (3, 3), (1, 3),
    (3, 1), (2, 0), (0, 2), (1, 2), (3, 2), (2, 1), (2, 3), (2, 2),
)
EARLY = 2
REST = 9
AHEAD = 8
RELAY_LAG = 1
HAND_LAG = 2
SENT_LAG = 4


def kernel(
    tok_hbm,
    routes_hbm,
    w_hbm,
    q_hbm,
    out_ref,
    routes,
    tok,
    wq,
    outbox,
    rows,
    places,
    acc,
    mom,
    tally,
    tally_in,
    tally_other,
    load_sem,
    a_send,
    a_recv,
    x_send,
    x_recv,
    f_send,
    f_recv,
    c_send,
    c_recv,
    t_send,
    t_recv,
    u_sem,
):
    dp, section, mp = lax.axis_index("dp"), lax.axis_index("section"), lax.axis_index("mp")
    y, z = dp // SIDE, dp % SIDE
    x_lo, core = mp // 2, mp % 2
    half = tok.shape[1]
    token_total = tok.shape[0]
    columns = w_hbm.shape[-1]

    across = (dp, 1 - section, (1 - x_lo) * 2 + core)
    beside = (dp, section, (1 - x_lo) * 2 + core)
    twin = (dp, section, x_lo * 2 + 1 - core)
    mine = jnp.where(section == x_lo, 0, PIECE)

    def shift(k):
        code = 0
        for i, (dy, dz) in enumerate(NEAREST):
            code = jnp.where(k % SHIFTS == i, dy * SIDE + dz, code)
        return ((y + code // SIDE) % SIDE) * SIDE + (z + code % SIDE) % SIDE

    def span(index, size):
        return pl.ds(pl.multiple_of(index * size, size), size)

    def remote(source, target, send, recv, device):
        return pltpu.make_async_remote_copy(source, target, send, recv, device, MESH)

    def a_copy(p):
        return remote(
            outbox.at[span(p, PIECE)],
            rows.at[core, span(p, PIECE)],
            a_send.at[p],
            a_recv.at[p],
            (shift(p), section, mp),
        )

    def t_copy(k):
        return remote(tally, tally_in.at[k], t_send.at[k], t_recv.at[k], (shift(k), section, mp))

    def u_copy():
        return remote(tally_in.at[0], tally_other, u_sem.at[0], u_sem.at[1], across)

    units = SHIFTS * PIECE // UNIT

    def x_copy(u):
        return remote(
            rows.at[core, span(u, UNIT)],
            rows.at[core, span(2 * units + u, UNIT)],
            x_send.at[u],
            x_recv.at[u],
            across,
        )

    def f_copy(u):
        return remote(
            rows.at[core, span(2 * units + u, UNIT)],
            rows.at[core, span(3 * units + u, UNIT)],
            f_send.at[u],
            f_recv.at[u],
            beside,
        )

    def c_copy(p, owner):
        return remote(
            rows.at[owner, span(p, PIECE)],
            rows.at[owner, span(p, PIECE)],
            c_send.at[p],
            c_recv.at[p],
            twin,
        )

    load_routes = pltpu.make_async_copy(routes_hbm, routes, load_sem.at[5])
    load_tok = pltpu.make_async_copy(
        tok_hbm.at[:, pl.ds(pl.multiple_of(core * half, half), half)], tok, load_sem.at[0]
    )
    loads = []
    for part in range(2):
        for i, source in enumerate((w_hbm, q_hbm)):
            loads.append(
                pltpu.make_async_copy(
                    source.at[0, 0, pl.ds(part * half, half)],
                    wq.at[part, :, pl.ds(i * columns, columns)],
                    load_sem.at[1 + 2 * part + i],
                )
            )
    load_routes.start()
    load_tok.start()

    barrier = pltpu.get_barrier_semaphore()
    for k in range(1, SHIFTS):
        pl.semaphore_signal(barrier, 1, device_id=(shift(k), section, mp), device_id_type=MESH)
    for peer in (across, beside, twin):
        pl.semaphore_signal(barrier, 1, device_id=peer, device_id_type=MESH)

    expert = lax.broadcasted_iota(jnp.int32, (SHIFTS, token_total), 0)
    before = lax.broadcasted_iota(jnp.int32, (token_total, token_total), 0)
    after = lax.broadcasted_iota(jnp.int32, (token_total, token_total), 1)
    upper = jnp.where(before <= after, 1.0, 0.0).astype(jnp.bfloat16)
    mom[...] = jnp.zeros_like(mom)
    load_routes.wait()
    chosen = jnp.zeros((SHIFTS, token_total), jnp.float32)
    for i in range(routes.shape[0]):
        chosen += jnp.where(routes[i : i + 1, :] == expert, 1.0, 0.0)
    rank = jnp.dot(chosen.astype(jnp.bfloat16), upper, preferred_element_type=jnp.float32)
    places[...] = jnp.where(chosen > 0, rank - 1.0, -1.0)
    tally[...] = jnp.broadcast_to(jnp.sum(chosen, axis=1, keepdims=True), tally.shape)
    load_tok.wait()

    slot = lax.broadcasted_iota(jnp.int32, (PIECE, token_total), 0)

    def collect(group):
        start = jnp.where(group < SIDE, mine, PIECE - mine)
        number = (slot + start).astype(jnp.float32)
        picks = []
        for j in range(SIDE):
            line = places[pl.ds(shift(group * SIDE + j), 1), :]
            picks.append(jnp.where(line == number, 1.0, 0.0).astype(jnp.bfloat16))
        pick = jnp.concatenate(picks, axis=0)
        outbox[span(group, GROUP), :] = jnp.dot(
            pick, tok[...], preferred_element_type=jnp.float32
        ).astype(jnp.bfloat16)

    def launch(p, ready):
        @pl.when(ready & (p % SHIFTS > 0) & (p < 2 * SHIFTS))
        def _():
            a_copy(p).start()

    def own_piece(p):
        rows[core, span(p, PIECE), :] = outbox[span(p, PIECE), :]

    def carry(p):
        for i in range(2):
            x_copy(2 * p + i).start()

    collect(0)
    pl.semaphore_wait(barrier, SHIFTS + 2)
    for p in range(1, SIDE):
        a_copy(p).start()
    own_piece(0)
    carry(0)
    c_copy(0, core).start()

    @pl.loop(1, 2 * SIDE)
    def _(group):
        collect(group)
        for j in range(SIDE):

            launch(group * SIDE + j, group * SIDE + j < AHEAD)

    own_piece(SHIFTS)
    c_copy(SHIFTS, core).start()
    for load in loads:
        load.start()
    for k in range(1, SHIFTS):
        t_copy(k).start()
    for load in loads:
        load.wait()

    def multiply(group):
        for j in range(SIDE):
            c_copy(group * SIDE + j, 1 - core).wait_recv()
        acc[...] = jnp.dot(
            rows[0, span(group, GROUP), :], wq[0], preferred_element_type=jnp.float32
        ) + jnp.dot(rows[1, span(group, GROUP), :], wq[1], preferred_element_type=jnp.float32)
        full = acc[:, :columns]
        quant = acc[:, columns:]

        def fold(values):
            return jnp.sum(values.reshape(GROUP // 8, 8, columns), axis=0)

        mom[0] += fold(quant * quant)
        mom[1] += fold(quant)
        mom[2] += fold(quant * full)
        mom[3] += fold(full)

    def sent(k):
        for p in (2 * k, 2 * k + 1):

            @pl.when(p % SHIFTS > 0)
            def _():
                a_copy(p).wait_send()

            x_copy(p).wait_send()
            f_copy(p).wait_send()
        c_copy(k, core).wait_send()
        c_copy(2 * SHIFTS + k, core).wait_send()
        c_copy(3 * SHIFTS + k, core).wait_send()

    def arrive(p):
        a_copy(p).wait_recv()
        carry(p)
        c_copy(p, core).start()

    for p in range(1, EARLY + 1):
        arrive(p)

    @pl.loop(0, STEPS)
    def _(step):
        for j in range(2):
            launch(AHEAD + 2 * step + j, True)

        @pl.when((step > 0) & (step + EARLY < SHIFTS))
        def _():
            arrive(step + EARLY)

        @pl.when((step >= RELAY_LAG) & (step < SHIFTS + RELAY_LAG))
        def _():
            k = step - RELAY_LAG
            for i in range(2):
                x_copy(2 * k + i).wait_recv()
                f_copy(2 * k + i).start()
            c_copy(2 * SHIFTS + k, core).start()

        @pl.when((step >= HAND_LAG) & (step < SHIFTS + HAND_LAG))
        def _():
            k = step - HAND_LAG
            for i in range(2):
                f_copy(2 * k + i).wait_recv()
            c_copy(3 * SHIFTS + k, core).start()

        @pl.when((step >= REST) & (step < REST + SHIFTS // 2))
        def _():
            for j in range(2):
                p = SHIFTS + 2 * (step - REST) + j

                @pl.when(p > SHIFTS)
                def _():
                    a_copy(p).wait_recv()
                    c_copy(p, core).start()

        for i in range(2):
            group = -1
            for at, groups in PRODUCTS.items():
                if len(groups) > i:
                    group = jnp.where(step == at, groups[i], group)
            pl.when(group >= 0)(functools.partial(multiply, group))

        @pl.when((step >= SENT_LAG) & (step < SHIFTS))
        def _():
            sent(step - SENT_LAG)

        @pl.when(step == SHIFTS // 2)
        def _():
            total = tally[...]
            for k in range(1, SHIFTS):
                t_copy(k).wait()
                total += tally_in[k]
            tally_in[0] = total
            u_copy().start()

    u_copy().wait()
    total = tally_in[0] + tally_other[...]
    named = lax.broadcasted_iota(jnp.int32, total.shape, 0)
    counts = jnp.sum(jnp.where(named == dp, total, 0.0), axis=0, keepdims=True)[:, :1]
    for i in range(4):
        out_ref[i : i + 1, :] = jnp.sum(mom[i], axis=0, keepdims=True)
    out_ref[4:, :] = jnp.broadcast_to(counts, (4, columns))

    for k in range(SHIFTS - SENT_LAG, SHIFTS):
        sent(k)
    for k in range(SHIFTS):
        c_copy(SHIFTS + k, core).wait_send()


def refit_columns(sums):
    square, first_moment, cross_term, target, counts = (sums[i] for i in range(5))
    denominator = counts + RIDGE
    diagonal = square + RIDGE
    anchored = cross_term + RIDGE
    determinant = diagonal * denominator - first_moment * first_moment
    refit_scale = (denominator * anchored - first_moment * target) / determinant
    refit_bias = (diagonal * target - first_moment * anchored) / determinant
    return refit_scale[None, None], refit_bias[None, None]


def local(tokens, routes, weight, quantized):
    token_total, width = tokens.shape
    columns = weight.shape[-1]
    vmem = pl.BlockSpec(memory_space=pltpu.VMEM)
    hbm = pl.BlockSpec(memory_space=pl.ANY)
    sems = pltpu.SemaphoreType.DMA
    sums = pl.pallas_call(
        kernel,
        out_shape=jax.ShapeDtypeStruct((8, columns), jnp.float32),
        in_specs=[hbm, hbm, hbm, hbm],
        out_specs=vmem,
        scratch_shapes=[
            pltpu.VMEM(routes.T.shape, jnp.int32),
            pltpu.VMEM((token_total, width // 2), jnp.bfloat16),
            pltpu.VMEM((2, width // 2, 2 * columns), jnp.bfloat16),
            pltpu.VMEM((SHIFTS * CAP, width // 2), jnp.bfloat16),
            pltpu.VMEM((2, 2 * SHIFTS * CAP, width // 2), jnp.bfloat16),
            pltpu.VMEM((SHIFTS, token_total), jnp.float32),
            pltpu.VMEM((GROUP, 2 * columns), jnp.float32),
            pltpu.VMEM((4, 8, columns), jnp.float32),
            pltpu.VMEM((SHIFTS, 128), jnp.float32),
            pltpu.VMEM((SHIFTS, SHIFTS, 128), jnp.float32),
            pltpu.VMEM((SHIFTS, 128), jnp.float32),
            sems((6,)),
        ]
        + [sems((2 * SHIFTS,))] * 6
        + [sems((4 * SHIFTS,))] * 2
        + [sems((SHIFTS,))] * 2
        + [sems((2,))],
        compiler_params=pltpu.CompilerParams(
            collective_id=0, has_side_effects=True, vmem_limit_bytes=56 << 20
        ),
        cost_estimate=pl.CostEstimate(
            flops=2 * 2048 * 4096 * 768, bytes_accessed=10 << 20, transcendentals=0
        ),
    )(tokens, routes.T, weight, quantized)
    return refit_columns(sums)


def solution(mesh):
    placed = (
        P(("dp", "section"), None),
        P(("dp", "section"), None),
        P("section", "dp", None, "mp"),
        P("section", "dp", None, "mp"),
    )
    return jax.shard_map(
        local,
        mesh=mesh,
        in_specs=placed,
        out_specs=(P("section", "dp", "mp"), P("section", "dp", "mp")),
        check_vma=False,
    )
```

time: 359 us -> 75.3 us (0.21); the launches traced: 354 us -> 75.1 us
  blocking collectives: 290 us -> 0 us
  Pallas kernels: 0 us -> 73 us
  matrix products: 29.7 us -> 0 us
  local copies, waits for them, and re-layouts: 18.7 us -> 0 us
  other arithmetic: 11.1 us -> 1.47 us
    psum x1 -> x0, blocking collectives: 187 us -> none  [local(): totals = lax.psum(local_counts, ('dp', 'section'))]
    all_to_all x1 -> x0, blocking collectives: 103 us -> none  [local(): lax.all_to_all(slot_rows, 'dp', split_axis=0, concat_axis=0, tiled=True)]
    pallas_call x0 -> x1, Pallas kernels: none -> 73 us  [local(): pl.pallas_call(kernel, out_shape=jax.ShapeDtypeStruct((8, columns), jnp.f...]
    dot_general x4 -> x0, matrix products: 29.7 us -> none  [the longest x2 15.8 us: column_sums(): jnp.einsum('sekd,edf->sekf', row_block, quant_block, preferred_element_ty...]
    gather x1 -> x0, local copies, waits for them, and re-layouts: 17.8 us -> none  [local(): tokens[row_index]]
    select_n x2 -> x0, other arithmetic: 7.22 us -> none  [the longest x1 7.22 us: local(): jnp.where(occupied[:, :, None], tokens[row_index], jnp.zeros((), tokens.d...]
  transfers between devices with their start and end apart: 1 -> 0, of which waited for: 0 -> 0; matrix products, arithmetic and copies ran while one was open for 4% -> 0% of each run, Pallas kernels for 0% -> 0%
where the time goes in v2:
time: 75.3 us; the launch traced here: 75.1 us
  Pallas kernels  73 us (97%)
  other arithmetic  1.47 us (2%)
    pallas_call x1, Pallas kernels, local(): pl.pallas_call(kernel, out_shape=jax.ShapeDtypeStruct((8, columns), jnp.f...  73 us

profile of v2, /device:TPU:1, one launch (start us, length us, event | category | flops | bytes accessed | tf_op | source)
XLA Modules:
  0.0 75.1 jit_solution(821180472567258666)
XLA Ops:
  0.6 73.0 %shard_map.59 = f32[8,384]{1,0:T(8,128)} custom-call(bf16[512,4096]{1,0:T(8,128)(2,1)} %tok_hbm.1, s32[8,512]{1,0:T(8,128)} %bitcast.5, bf16[1,1,4096,384]{3,2,1,0:T(8,128)(2,1)} %w_hbm.1, bf16[1,1,4096,384]{3,2,1,0:T(8,128)(2,1)} %q_hbm.1), custom_call_target="tpu_custom_call" | custom-call | flops 12884901888 | bytes 10485760 | tf_op jit(solution)/shard_map/pallas_call | solution.py:343
  73.6 1.5 %fusion.1 = (f32[1,1,384]{2,1,0:T(1,128)}, f32[1,1,384]{2,1,0:T(1,128)}) fusion(f32[8,384]{1,0:T(8,128)} %shard_map.59), kind=kLoop, calls=%fused_computation.7 | loop fusion | flops 5376 | bytes 10752 | tf_op jit(solution)/shard_map/div | solution.py:333

commit v3 on v2

--- a/solution.py
+++ b/solution.py
@@ -16,20 +16,22 @@
 UNIT = PIECE // 2
 GROUP = SIDE * PIECE
 PRODUCTS = {
-    2: (0,), 5: (8,), 6: (1,), 7: (12,), 9: (9,), 10: (2,), 11: (13,), 12: (4,), 13: (10,),
-    14: (3, 5), 15: (14,), 16: (6,), 17: (11, 7), 18: (15,),
+    2: (0,), 5: (8,), 6: (1,), 8: (12,), 9: (9,), 10: (2,), 11: (13,), 13: (10, 4),
+    14: (3,), 15: (5,), 16: (14,), 17: (6, 11), 19: (15, 7),
 }
-STEPS = 19
+STEPS = 20
 NEAREST = (
     (0, 0), (1, 0), (0, 1), (3, 0), (0, 3), (1, 1), (3, 3), (1, 3),
-    (3, 1), (2, 0), (0, 2), (1, 2), (3, 2), (2, 1), (2, 3), (2, 2),
+    (3, 1), (2, 0), (0, 2), (1, 2), (2, 1), (3, 2), (2, 3), (2, 2),
 )
+SHIFT_ORDER = NEAREST + NEAREST
 EARLY = 2
-REST = 9
+REST = 11
 AHEAD = 8
+STEPS_SEND = (2 * SHIFTS - AHEAD) // 2
 RELAY_LAG = 1
-HAND_LAG = 2
-SENT_LAG = 4
+HAND_LAG = 3
+SENT_LAG = 5
 
 
 def kernel(
@@ -76,8 +78,8 @@
 
     def shift(k):
         code = 0
-        for i, (dy, dz) in enumerate(NEAREST):
-            code = jnp.where(k % SHIFTS == i, dy * SIDE + dz, code)
+        for i, (dy, dz) in enumerate(SHIFT_ORDER):
+            code = jnp.where(k == i, dy * SIDE + dz, code)
         return ((y + code // SIDE) % SIDE) * SIDE + (z + code % SIDE) % SIDE
 
     def span(index, size):
@@ -193,6 +195,8 @@
         for i in range(2):
             x_copy(2 * p + i).start()
 
+    for load in loads:
+        load.start()
     collect(0)
     pl.semaphore_wait(barrier, SHIFTS + 2)
     for p in range(1, SIDE):
@@ -201,34 +205,31 @@
     carry(0)
     c_copy(0, core).start()
 
-    @pl.loop(1, 2 * SIDE)
+    @pl.loop(1, AHEAD // SIDE)
     def _(group):
         collect(group)
         for j in range(SIDE):
-
-            launch(group * SIDE + j, group * SIDE + j < AHEAD)
-
-    own_piece(SHIFTS)
-    c_copy(SHIFTS, core).start()
-    for load in loads:
-        load.start()
+            launch(group * SIDE + j, True)
+
+    collect(AHEAD // SIDE)
     for k in range(1, SHIFTS):
         t_copy(k).start()
-    for load in loads:
-        load.wait()
-
-    def multiply(group):
+
+    def part(group, i):
+        return jnp.dot(rows[i, span(group, GROUP), :], wq[i], preferred_element_type=jnp.float32)
+
+    def fold(values):
+        return jnp.sum(values.reshape(GROUP // 8, 8, columns), axis=0)
+
+    def begin(group):
         for j in range(SIDE):
             c_copy(group * SIDE + j, 1 - core).wait_recv()
-        acc[...] = jnp.dot(
-            rows[0, span(group, GROUP), :], wq[0], preferred_element_type=jnp.float32
-        ) + jnp.dot(rows[1, span(group, GROUP), :], wq[1], preferred_element_type=jnp.float32)
+        acc[...] = part(group, 0)
+
+    def finish(group):
+        acc[...] += part(group, 1)
         full = acc[:, :columns]
         quant = acc[:, columns:]
-
-        def fold(values):
-            return jnp.sum(values.reshape(GROUP // 8, 8, columns), axis=0)
-
         mom[0] += fold(quant * quant)
         mom[1] += fold(quant)
         mom[2] += fold(quant * full)
@@ -255,22 +256,43 @@
     for p in range(1, EARLY + 1):
         arrive(p)
 
+    def product(step, i):
+        group = -1
+        for at, groups in PRODUCTS.items():
+            if len(groups) > i:
+                group = jnp.where(step == at, groups[i], group)
+        return group
+
     @pl.loop(0, STEPS)
     def _(step):
+        first, second = product(step, 0), product(step, 1)
+
+        def relay(u):
+            @pl.when((step >= RELAY_LAG) & (step < SHIFTS + RELAY_LAG))
+            def _():
+                x_copy(u).wait_recv()
+                f_copy(u).start()
+
+        relay(2 * (step - RELAY_LAG))
         for j in range(2):
             launch(AHEAD + 2 * step + j, True)
 
+        @pl.when(step == min(PRODUCTS))
+        def _():
+            for load in loads:
+                load.wait()
+
+        pl.when(first >= 0)(functools.partial(begin, first))
+
         @pl.when((step > 0) & (step + EARLY < SHIFTS))
         def _():
             arrive(step + EARLY)
 
+        relay(2 * (step - RELAY_LAG) + 1)
+
         @pl.when((step >= RELAY_LAG) & (step < SHIFTS + RELAY_LAG))
         def _():
-            k = step - RELAY_LAG
-            for i in range(2):
-                x_copy(2 * k + i).wait_recv()
-                f_copy(2 * k + i).start()
-            c_copy(2 * SHIFTS + k, core).start()
+            c_copy(2 * SHIFTS + step - RELAY_LAG, core).start()
 
         @pl.when((step >= HAND_LAG) & (step < SHIFTS + HAND_LAG))
         def _():
@@ -279,6 +301,23 @@
                 f_copy(2 * k + i).wait_recv()
             c_copy(3 * SHIFTS + k, core).start()
 
+        @pl.when((step % 2 == 1) & (step < STEPS_SEND - 2))
+        def _():
+            group = AHEAD // SIDE + (step + 1) // 2
+            collect(group)
+
+            @pl.when(group == SIDE)
+            def _():
+                own_piece(SHIFTS)
+                c_copy(SHIFTS, core).start()
+
+        pl.when(first >= 0)(functools.partial(finish, first))
+
+        @pl.when(second >= 0)
+        def _():
+            begin(second)
+            finish(second)
+
         @pl.when((step >= REST) & (step < REST + SHIFTS // 2))
         def _():
             for j in range(2):
@@ -288,13 +327,6 @@
                 def _():
                     a_copy(p).wait_recv()
                     c_copy(p, core).start()
-
-        for i in range(2):
-            group = -1
-            for at, groups in PRODUCTS.items():
-                if len(groups) > i:
-                    group = jnp.where(step == at, groups[i], group)
-            pl.when(group >= 0)(functools.partial(multiply, group))
 
         @pl.when((step >= SENT_LAG) & (step < SHIFTS))
         def _():

time: 75.3 us -> 72.1 us (0.958)
  Pallas kernels: 73 us -> 69.8 us
    pallas_call x1, Pallas kernels: 73 us -> 69.8 us  [local(): pl.pallas_call(kernel, out_shape=jax.ShapeDtypeStruct((8, columns), jnp.f...]
where the time goes in v3:
time: 72.1 us; the launch traced here: 71.9 us
  Pallas kernels  69.8 us (97%)
  other arithmetic  1.47 us (2%)
    pallas_call x1, Pallas kernels, local(): pl.pallas_call(kernel, out_shape=jax.ShapeDtypeStruct((8, columns), jnp.f...  69.8 us
    div x1, other arithmetic, refit_columns(): refit_bias = (diagonal * target - first_moment * anchored) / determinant  1.47 us

profile of v3, /device:TPU:1, one launch (start us, length us, event | category | flops | bytes accessed | tf_op | source)
XLA Modules:
  0.0 71.9 jit_solution(2025052858804450098)
XLA Ops:
  0.6 69.8 %shard_map.59 = f32[8,384]{1,0:T(8,128)} custom-call(bf16[512,4096]{1,0:T(8,128)(2,1)} %tok_hbm.1, s32[8,512]{1,0:T(8,128)} %bitcast.5, bf16[1,1,4096,384]{3,2,1,0:T(8,128)(2,1)} %w_hbm.1, bf16[1,1,4096,384]{3,2,1,0:T(8,128)(2,1)} %q_hbm.1), custom_call_target="tpu_custom_call" | custom-call | flops 12884901888 | bytes 10485760 | tf_op jit(solution)/shard_map/pallas_call | solution.py:375
  70.4 1.5 %fusion.1 = (f32[1,1,384]{2,1,0:T(1,128)}, f32[1,1,384]{2,1,0:T(1,128)}) fusion(f32[8,384]{1,0:T(8,128)} %shard_map.59), kind=kLoop, calls=%fused_computation.7 | loop fusion | flops 5376 | bytes 10752 | tf_op jit(solution)/shard_map/div | solution.py:365

commit v4 on v3

--- a/solution.py
+++ b/solution.py
@@ -17,7 +17,7 @@
 GROUP = SIDE * PIECE
 PRODUCTS = {
     2: (0,), 5: (8,), 6: (1,), 8: (12,), 9: (9,), 10: (2,), 11: (13,), 13: (10, 4),
-    14: (3,), 15: (5,), 16: (14,), 17: (6, 11), 19: (15, 7),
+    14: (3,), 15: (5,), 16: (14,), 17: (6, 11), 19: (7, 15),
 }
 STEPS = 20
 NEAREST = (
@@ -31,7 +31,6 @@
 STEPS_SEND = (2 * SHIFTS - AHEAD) // 2
 RELAY_LAG = 1
 HAND_LAG = 3
-SENT_LAG = 5
 
 
 def kernel(
@@ -60,8 +59,7 @@
     f_recv,
     c_send,
     c_recv,
-    t_send,
-    t_recv,
+    t_sem,
     u_sem,
 ):
     dp, section, mp = lax.axis_index("dp"), lax.axis_index("section"), lax.axis_index("mp")
@@ -77,9 +75,12 @@
     mine = jnp.where(section == x_lo, 0, PIECE)
 
     def shift(k):
-        code = 0
-        for i, (dy, dz) in enumerate(SHIFT_ORDER):
-            code = jnp.where(k == i, dy * SIDE + dz, code)
+        if isinstance(k, int):
+            code = SHIFT_ORDER[k][0] * SIDE + SHIFT_ORDER[k][1]
+        else:
+            code = 0
+            for i, (dy, dz) in enumerate(SHIFT_ORDER):
+                code = jnp.where(k == i, dy * SIDE + dz, code)
         return ((y + code // SIDE) % SIDE) * SIDE + (z + code % SIDE) % SIDE
 
     def span(index, size):
@@ -92,13 +93,13 @@
         return remote(
             outbox.at[span(p, PIECE)],
             rows.at[core, span(p, PIECE)],
-            a_send.at[p],
-            a_recv.at[p],
+            a_send.at[0],
+            a_recv.at[jnp.where(p < SHIFTS, p, SHIFTS + (p - SHIFTS) // 2)],
             (shift(p), section, mp),
         )
 
     def t_copy(k):
-        return remote(tally, tally_in.at[k], t_send.at[k], t_recv.at[k], (shift(k), section, mp))
+        return remote(tally, tally_in.at[k], t_sem.at[0], t_sem.at[1], (shift(k), section, mp))
 
     def u_copy():
         return remote(tally_in.at[0], tally_other, u_sem.at[0], u_sem.at[1], across)
@@ -109,7 +110,7 @@
         return remote(
             rows.at[core, span(u, UNIT)],
             rows.at[core, span(2 * units + u, UNIT)],
-            x_send.at[u],
+            x_send.at[0],
             x_recv.at[u],
             across,
         )
@@ -118,21 +119,25 @@
         return remote(
             rows.at[core, span(2 * units + u, UNIT)],
             rows.at[core, span(3 * units + u, UNIT)],
-            f_send.at[u],
-            f_recv.at[u],
+            f_send.at[0],
+            f_recv.at[u // 2],
             beside,
         )
 
-    def c_copy(p, owner):
+    def c_copy(p, size=PIECE):
+        place = pl.ds(pl.multiple_of(p * PIECE, PIECE), size)
         return remote(
-            rows.at[owner, span(p, PIECE)],
-            rows.at[owner, span(p, PIECE)],
-            c_send.at[p],
-            c_recv.at[p],
+            rows.at[core, place],
+            rows.at[core, place],
+            c_send.at[0],
+            c_recv.at[p // SIDE],
             twin,
         )
 
-    load_routes = pltpu.make_async_copy(routes_hbm, routes, load_sem.at[5])
+    def await_bytes(ref, sem):
+        pltpu.make_async_copy(ref, ref, sem).wait()
+
+    load_routes = pltpu.make_async_copy(routes_hbm, routes, load_sem.at[2])
     load_tok = pltpu.make_async_copy(
         tok_hbm.at[:, pl.ds(pl.multiple_of(core * half, half), half)], tok, load_sem.at[0]
     )
@@ -143,7 +148,7 @@
                 pltpu.make_async_copy(
                     source.at[0, 0, pl.ds(part * half, half)],
                     wq.at[part, :, pl.ds(i * columns, columns)],
-                    load_sem.at[1 + 2 * part + i],
+                    load_sem.at[1],
                 )
             )
     load_routes.start()
@@ -203,7 +208,7 @@
         a_copy(p).start()
     own_piece(0)
     carry(0)
-    c_copy(0, core).start()
+    c_copy(0).start()
 
     @pl.loop(1, AHEAD // SIDE)
     def _(group):
@@ -222,8 +227,7 @@
         return jnp.sum(values.reshape(GROUP // 8, 8, columns), axis=0)
 
     def begin(group):
-        for j in range(SIDE):
-            c_copy(group * SIDE + j, 1 - core).wait_recv()
+        await_bytes(rows.at[1 - core, span(group, GROUP)], c_recv.at[group])
         acc[...] = part(group, 0)
 
     def finish(group):
@@ -235,23 +239,10 @@
         mom[2] += fold(quant * full)
         mom[3] += fold(full)
 
-    def sent(k):
-        for p in (2 * k, 2 * k + 1):
-
-            @pl.when(p % SHIFTS > 0)
-            def _():
-                a_copy(p).wait_send()
-
-            x_copy(p).wait_send()
-            f_copy(p).wait_send()
-        c_copy(k, core).wait_send()
-        c_copy(2 * SHIFTS + k, core).wait_send()
-        c_copy(3 * SHIFTS + k, core).wait_send()
-
     def arrive(p):
         a_copy(p).wait_recv()
         carry(p)
-        c_copy(p, core).start()
+        c_copy(p).start()
 
     for p in range(1, EARLY + 1):
         arrive(p)
@@ -279,8 +270,7 @@
 
         @pl.when(step == min(PRODUCTS))
         def _():
-            for load in loads:
-                load.wait()
+            await_bytes(wq, load_sem.at[1])
 
         pl.when(first >= 0)(functools.partial(begin, first))
 
@@ -292,14 +282,13 @@
 
         @pl.when((step >= RELAY_LAG) & (step < SHIFTS + RELAY_LAG))
         def _():
-            c_copy(2 * SHIFTS + step - RELAY_LAG, core).start()
+            c_copy(2 * SHIFTS + step - RELAY_LAG).start()
 
         @pl.when((step >= HAND_LAG) & (step < SHIFTS + HAND_LAG))
         def _():
             k = step - HAND_LAG
-            for i in range(2):
-                f_copy(2 * k + i).wait_recv()
-            c_copy(3 * SHIFTS + k, core).start()
+            await_bytes(rows.at[core, span(3 * SHIFTS + k, PIECE)], f_recv.at[k])
+            c_copy(3 * SHIFTS + k).start()
 
         @pl.when((step % 2 == 1) & (step < STEPS_SEND - 2))
         def _():
@@ -309,7 +298,7 @@
             @pl.when(group == SIDE)
             def _():
                 own_piece(SHIFTS)
-                c_copy(SHIFTS, core).start()
+                c_copy(SHIFTS).start()
 
         pl.when(first >= 0)(functools.partial(finish, first))
 
@@ -318,25 +307,25 @@
             begin(second)
             finish(second)
 
-        @pl.when((step >= REST) & (step < REST + SHIFTS // 2))
-        def _():
-            for j in range(2):
-                p = SHIFTS + 2 * (step - REST) + j
-
-                @pl.when(p > SHIFTS)
-                def _():
-                    a_copy(p).wait_recv()
-                    c_copy(p, core).start()
-
-        @pl.when((step >= SENT_LAG) & (step < SHIFTS))
-        def _():
-            sent(step - SENT_LAG)
+        @pl.when(step == REST)
+        def _():
+            a_copy(SHIFTS + 1).wait_recv()
+            c_copy(SHIFTS + 1).start()
+
+        @pl.when((step > REST) & (step < REST + SHIFTS // 2))
+        def _():
+            p = SHIFTS + 2 * (step - REST)
+            await_bytes(
+                rows.at[core, pl.ds(pl.multiple_of(p * PIECE, PIECE), 2 * PIECE)],
+                a_recv.at[SHIFTS + step - REST],
+            )
+            c_copy(p, 2 * PIECE).start()
 
         @pl.when(step == SHIFTS // 2)
         def _():
+            await_bytes(tally_in.at[pl.ds(1, SHIFTS - 1)], t_sem.at[1])
             total = tally[...]
             for k in range(1, SHIFTS):
-                t_copy(k).wait()
                 total += tally_in[k]
             tally_in[0] = total
             u_copy().start()
@@ -349,10 +338,11 @@
         out_ref[i : i + 1, :] = jnp.sum(mom[i], axis=0, keepdims=True)
     out_ref[4:, :] = jnp.broadcast_to(counts, (4, columns))
 
-    for k in range(SHIFTS - SENT_LAG, SHIFTS):
-        sent(k)
-    for k in range(SHIFTS):
-        c_copy(SHIFTS + k, core).wait_send()
+    await_bytes(outbox.at[pl.ds(0, (SHIFTS - 1) * CAP)], a_send.at[0])
+    await_bytes(tally_in.at[pl.ds(1, SHIFTS - 1)], t_sem.at[0])
+    await_bytes(rows.at[0, pl.ds(0, SHIFTS * PIECE)], x_send.at[0])
+    await_bytes(rows.at[0, pl.ds(0, SHIFTS * PIECE)], f_send.at[0])
+    await_bytes(rows.at[0], c_send.at[0])
 
 
 def refit_columns(sums):
@@ -389,12 +379,18 @@
             pltpu.VMEM((SHIFTS, 128), jnp.float32),
             pltpu.VMEM((SHIFTS, SHIFTS, 128), jnp.float32),
             pltpu.VMEM((SHIFTS, 128), jnp.float32),
-            sems((6,)),
-        ]
-        + [sems((2 * SHIFTS,))] * 6
-        + [sems((4 * SHIFTS,))] * 2
-        + [sems((SHIFTS,))] * 2
-        + [sems((2,))],
+            sems((3,)),
+            sems((1,)),
+            sems((SHIFTS + SHIFTS // 2,)),
+            sems((1,)),
+            sems((2 * SHIFTS,)),
+            sems((1,)),
+            sems((SHIFTS,)),
+            sems((1,)),
+            sems((SHIFTS,)),
+            sems((2,)),
+            sems((2,)),
+        ],
         compiler_params=pltpu.CompilerParams(
             collective_id=0, has_side_effects=True, vmem_limit_bytes=56 << 20
         ),

time: 72.1 us -> 70.1 us (0.972)
  Pallas kernels: 69.8 us -> 67.7 us
    pallas_call x1, Pallas kernels: 69.8 us -> 67.7 us  [local(): pl.pallas_call(kernel, out_shape=jax.ShapeDtypeStruct((8, columns), jnp.f...]
where the time goes in v4:
time: 70.1 us; the launch traced here: 69.9 us
  Pallas kernels  67.7 us (97%)
  other arithmetic  1.47 us (2%)
    pallas_call x1, Pallas kernels, local(): pl.pallas_call(kernel, out_shape=jax.ShapeDtypeStruct((8, columns), jnp.f...  67.7 us
    div x1, other arithmetic, refit_columns(): refit_bias = (diagonal * target - first_moment * anchored) / determinant  1.47 us

profile of v4, /device:TPU:1, one launch (start us, length us, event | category | flops | bytes accessed | tf_op | source)
XLA Modules:
  0.0 69.9 jit_solution(17428187245126806625)
XLA Ops:
  0.6 67.7 %shard_map.59 = f32[8,384]{1,0:T(8,128)} custom-call(bf16[512,4096]{1,0:T(8,128)(2,1)} %tok_hbm.1, s32[8,512]{1,0:T(8,128)} %bitcast.5, bf16[1,1,4096,384]{3,2,1,0:T(8,128)(2,1)} %w_hbm.1, bf16[1,1,4096,384]{3,2,1,0:T(8,128)(2,1)} %q_hbm.1), custom_call_target="tpu_custom_call" | custom-call | flops 12884901888 | bytes 10485760 | tf_op jit(solution)/shard_map/pallas_call | solution.py:365
  68.4 1.5 %fusion.1 = (f32[1,1,384]{2,1,0:T(1,128)}, f32[1,1,384]{2,1,0:T(1,128)}) fusion(f32[8,384]{1,0:T(8,128)} %shard_map.59), kind=kLoop, calls=%fused_computation.7 | loop fusion | flops 5376 | bytes 10752 | tf_op jit(solution)/shard_map/div | solution.py:355

commit v5 on v4

--- a/solution.py
+++ b/solution.py
@@ -272,41 +272,6 @@
         def _():
             await_bytes(wq, load_sem.at[1])
 
-        pl.when(first >= 0)(functools.partial(begin, first))
-
-        @pl.when((step > 0) & (step + EARLY < SHIFTS))
-        def _():
-            arrive(step + EARLY)
-
-        relay(2 * (step - RELAY_LAG) + 1)
-
-        @pl.when((step >= RELAY_LAG) & (step < SHIFTS + RELAY_LAG))
-        def _():
-            c_copy(2 * SHIFTS + step - RELAY_LAG).start()
-
-        @pl.when((step >= HAND_LAG) & (step < SHIFTS + HAND_LAG))
-        def _():
-            k = step - HAND_LAG
-            await_bytes(rows.at[core, span(3 * SHIFTS + k, PIECE)], f_recv.at[k])
-            c_copy(3 * SHIFTS + k).start()
-
-        @pl.when((step % 2 == 1) & (step < STEPS_SEND - 2))
-        def _():
-            group = AHEAD // SIDE + (step + 1) // 2
-            collect(group)
-
-            @pl.when(group == SIDE)
-            def _():
-                own_piece(SHIFTS)
-                c_copy(SHIFTS).start()
-
-        pl.when(first >= 0)(functools.partial(finish, first))
-
-        @pl.when(second >= 0)
-        def _():
-            begin(second)
-            finish(second)
-
         @pl.when(step == REST)
         def _():
             a_copy(SHIFTS + 1).wait_recv()
@@ -320,6 +285,41 @@
                 a_recv.at[SHIFTS + step - REST],
             )
             c_copy(p, 2 * PIECE).start()
+
+        pl.when(first >= 0)(functools.partial(begin, first))
+
+        @pl.when((step > 0) & (step + EARLY < SHIFTS))
+        def _():
+            arrive(step + EARLY)
+
+        relay(2 * (step - RELAY_LAG) + 1)
+
+        @pl.when((step >= RELAY_LAG) & (step < SHIFTS + RELAY_LAG))
+        def _():
+            c_copy(2 * SHIFTS + step - RELAY_LAG).start()
+
+        @pl.when((step >= HAND_LAG) & (step < SHIFTS + HAND_LAG))
+        def _():
+            k = step - HAND_LAG
+            await_bytes(rows.at[core, span(3 * SHIFTS + k, PIECE)], f_recv.at[k])
+            c_copy(3 * SHIFTS + k).start()
+
+        @pl.when((step % 2 == 1) & (step < STEPS_SEND - 2))
+        def _():
+            group = AHEAD // SIDE + (step + 1) // 2
+            collect(group)
+
+            @pl.when(group == SIDE)
+            def _():
+                own_piece(SHIFTS)
+                c_copy(SHIFTS).start()
+
+        pl.when(first >= 0)(functools.partial(finish, first))
+
+        @pl.when(second >= 0)
+        def _():
+            begin(second)
+            finish(second)
 
         @pl.when(step == SHIFTS // 2)
         def _():

time: 70.1 us -> 69 us (0.984)
  Pallas kernels: 67.7 us -> 66.7 us
    pallas_call x1, Pallas kernels: 67.7 us -> 66.7 us  [local(): pl.pallas_call(kernel, out_shape=jax.ShapeDtypeStruct((8, columns), jnp.f...]
where the time goes in v5:
time: 69 us; the launch traced here: 68.8 us
  Pallas kernels  66.7 us (97%)
  other arithmetic  1.47 us (2%)
    pallas_call x1, Pallas kernels, local(): pl.pallas_call(kernel, out_shape=jax.ShapeDtypeStruct((8, columns), jnp.f...  66.7 us
    div x1, other arithmetic, refit_columns(): refit_bias = (diagonal * target - first_moment * anchored) / determinant  1.47 us

profile of v5, /device:TPU:1, one launch (start us, length us, event | category | flops | bytes accessed | tf_op | source)
XLA Modules:
  0.0 68.8 jit_solution(12858557159111989269)
XLA Ops:
  0.6 66.7 %shard_map.59 = f32[8,384]{1,0:T(8,128)} custom-call(bf16[512,4096]{1,0:T(8,128)(2,1)} %tok_hbm.1, s32[8,512]{1,0:T(8,128)} %bitcast.5, bf16[1,1,4096,384]{3,2,1,0:T(8,128)(2,1)} %w_hbm.1, bf16[1,1,4096,384]{3,2,1,0:T(8,128)(2,1)} %q_hbm.1), custom_call_target="tpu_custom_call" | custom-call | flops 12884901888 | bytes 10485760 | tf_op jit(solution)/shard_map/pallas_call | solution.py:365
  67.3 1.5 %fusion.1 = (f32[1,1,384]{2,1,0:T(1,128)}, f32[1,1,384]{2,1,0:T(1,128)}) fusion(f32[8,384]{1,0:T(8,128)} %shard_map.59), kind=kLoop, calls=%fused_computation.7 | loop fusion | flops 5376 | bytes 10752 | tf_op jit(solution)/shard_map/div | solution.py:355

commit v6 on v5

--- a/solution.py
+++ b/solution.py
@@ -26,6 +26,7 @@
 )
 SHIFT_ORDER = NEAREST + NEAREST
 EARLY = 2
+PARTS = 4
 REST = 11
 AHEAD = 8
 STEPS_SEND = (2 * SHIFTS - AHEAD) // 2
@@ -124,15 +125,14 @@
             beside,
         )
 
-    def c_copy(p, size=PIECE):
-        place = pl.ds(pl.multiple_of(p * PIECE, PIECE), size)
-        return remote(
-            rows.at[core, place],
-            rows.at[core, place],
-            c_send.at[0],
-            c_recv.at[p // SIDE],
-            twin,
-        )
+    def c_copy(p, size=PIECE, parts=1):
+        for i in range(parts):
+            place = rows.at[
+                core,
+                pl.ds(pl.multiple_of(p * PIECE, PIECE), size),
+                pl.ds(i * half // parts, half // parts),
+            ]
+            remote(place, place, c_send.at[0], c_recv.at[p // SIDE], twin).start()
 
     def await_bytes(ref, sem):
         pltpu.make_async_copy(ref, ref, sem).wait()
@@ -208,7 +208,7 @@
         a_copy(p).start()
     own_piece(0)
     carry(0)
-    c_copy(0).start()
+    c_copy(0)
 
     @pl.loop(1, AHEAD // SIDE)
     def _(group):
@@ -242,7 +242,7 @@
     def arrive(p):
         a_copy(p).wait_recv()
         carry(p)
-        c_copy(p).start()
+        c_copy(p)
 
     for p in range(1, EARLY + 1):
         arrive(p)
@@ -275,7 +275,7 @@
         @pl.when(step == REST)
         def _():
             a_copy(SHIFTS + 1).wait_recv()
-            c_copy(SHIFTS + 1).start()
+            c_copy(SHIFTS + 1)
 
         @pl.when((step > REST) & (step < REST + SHIFTS // 2))
         def _():
@@ -284,7 +284,7 @@
                 rows.at[core, pl.ds(pl.multiple_of(p * PIECE, PIECE), 2 * PIECE)],
                 a_recv.at[SHIFTS + step - REST],
             )
-            c_copy(p, 2 * PIECE).start()
+            c_copy(p, 2 * PIECE, 2 * PARTS)
 
         pl.when(first >= 0)(functools.partial(begin, first))
 
@@ -296,13 +296,13 @@
 
         @pl.when((step >= RELAY_LAG) & (step < SHIFTS + RELAY_LAG))
         def _():
-            c_copy(2 * SHIFTS + step - RELAY_LAG).start()
+            c_copy(2 * SHIFTS + step - RELAY_LAG, PIECE, PARTS)
 
         @pl.when((step >= HAND_LAG) & (step < SHIFTS + HAND_LAG))
         def _():
             k = step - HAND_LAG
             await_bytes(rows.at[core, span(3 * SHIFTS + k, PIECE)], f_recv.at[k])
-            c_copy(3 * SHIFTS + k).start()
+            c_copy(3 * SHIFTS + k, PIECE, PARTS)
 
         @pl.when((step % 2 == 1) & (step < STEPS_SEND - 2))
         def _():
@@ -312,7 +312,7 @@
             @pl.when(group == SIDE)
             def _():
                 own_piece(SHIFTS)
-                c_copy(SHIFTS).start()
+                c_copy(SHIFTS)
 
         pl.when(first >= 0)(functools.partial(finish, first))
 

time: 69 us -> 69.1 us (level)
  no operation moved by 1% of the time
where the time goes in v6:
time: 69.1 us; the launch traced here: 68.8 us
  Pallas kernels  66.7 us (97%)
  other arithmetic  1.47 us (2%)
    pallas_call x1, Pallas kernels, local(): pl.pallas_call(kernel, out_shape=jax.ShapeDtypeStruct((8, columns), jnp.f...  66.7 us
    div x1, other arithmetic, refit_columns(): refit_bias = (diagonal * target - first_moment * anchored) / determinant  1.47 us

profile of v6, /device:TPU:1, one launch (start us, length us, event | category | flops | bytes accessed | tf_op | source)
XLA Modules:
  0.0 68.8 jit_solution(18045947563893192560)
XLA Ops:
  0.6 66.7 %shard_map.59 = f32[8,384]{1,0:T(8,128)} custom-call(bf16[512,4096]{1,0:T(8,128)(2,1)} %tok_hbm.1, s32[8,512]{1,0:T(8,128)} %bitcast.5, bf16[1,1,4096,384]{3,2,1,0:T(8,128)(2,1)} %w_hbm.1, bf16[1,1,4096,384]{3,2,1,0:T(8,128)(2,1)} %q_hbm.1), custom_call_target="tpu_custom_call" | custom-call | flops 12884901888 | bytes 10485760 | tf_op jit(solution)/shard_map/pallas_call | solution.py:365
  67.3 1.5 %fusion.1 = (f32[1,1,384]{2,1,0:T(1,128)}, f32[1,1,384]{2,1,0:T(1,128)}) fusion(f32[8,384]{1,0:T(8,128)} %shard_map.59), kind=kLoop, calls=%fused_computation.7 | loop fusion | flops 5376 | bytes 10752 | tf_op jit(solution)/shard_map/div | solution.py:355
